TPU v7x, 32 devices: a whole 2x2x4 slice. The times are simulated.
32 devices in a mesh: own: 8 (over z, y), red: 4 (over x, core).
Axes of the slice: x: 2, y: 2, z: 4, core: 2. Of those that a mesh axis runs over, the one named last changes fastest.
Arguments:
- amp_tiles: bfloat16 [2048, 128, 128], P(('own', 'red')), may hold values from -6 to 6
- int_tiles: bfloat16 [2048, 128, 128], P(('own', 'red')), may hold values from -0.0625 to 0.0625
- requests: int32 [8, 4, 8, 2, 8], P('own', 'red'), may hold values from -1 to 63, as said below
- tri_amp: int32 [256, 4, 64], P('own', 'red'), may hold values from 0 to 63, as said below
- tri_int: int32 [256, 4, 64], P('own', 'red'), may hold values from 0 to 63, as said below
- tri_count: int32 [256, 4], P('own', 'red'), may hold values from 1 to 64, as said below
Outputs:
- residual: float32 [256, 128, 128], P(('own', 'red'))
Inputs may be any that keep to these rules, and one draw needn't show every extreme that they name: -1 marks an empty slot and live slots come first; the live numbers in one row of 8 slots are distinct; every owner device has 8 live amplitude requests to some holder and 8 live integral requests to some holder. tri_amp[t, r, k] // 8 is a holder h and tri_amp[t, r, k] % 8 is below the number of live amplitude requests of the owner of t, on red index r, to h. `tri_int`: likewise for the integral requests. `tri_count`: on every owner and red index some residual tile has 64 live triples.
All inputs are finite; a program needn't handle non-finite values.
Results may differ from a plain program's by a relative error of at most 0.0003.
Values may be sent and summed in bfloat16 or wider, within the bound.
A program may use at most 128 MiB of HBM per device.

v0:
```python
import math

import jax
import jax.numpy as jnp
from jax import lax
from jax.sharding import PartitionSpec as P


def select_tiles(store, wanted):
    clipped = jnp.clip(wanted, 0, store.shape[0] - 1)
    picked = store[clipped]
    return jnp.where((wanted >= 0)[:, :, None, None], picked, jnp.zeros((), store.dtype))


def contract_rows(got_amp, got_int, amp_pos, int_pos, counts):
    row_count, slot_count = amp_pos.shape
    received = got_amp.shape[0]
    tile_width = got_amp.shape[-1]
    block_rows = math.gcd(8, row_count)
    keep_mask = lax.broadcasted_iota(jnp.int32, (row_count, slot_count), 1) < counts[:, None]
    flat_amp = got_amp.reshape(received, tile_width * tile_width)
    flat_int = got_int.reshape(received, tile_width * tile_width)
    slot_iota = lax.broadcasted_iota(jnp.int32, (1, 1, received), 2)

    def one_block(operands):
        block_amp, block_int, block_keep = operands
        pick_amp = ((block_amp[:, :, None] == slot_iota) & block_keep[:, :, None]).astype(
            got_amp.dtype
        )
        pick_int = (block_int[:, :, None] == slot_iota).astype(got_int.dtype)
        left_tiles = jnp.einsum(
            "nkm,mx->nkx", pick_amp, flat_amp, preferred_element_type=jnp.float32
        ).astype(got_amp.dtype)
        right_tiles = jnp.einsum(
            "nkm,mx->nkx", pick_int, flat_int, preferred_element_type=jnp.float32
        ).astype(got_int.dtype)
        left_tiles = left_tiles.reshape(block_rows, slot_count, tile_width, tile_width)
        right_tiles = right_tiles.reshape(block_rows, slot_count, tile_width, tile_width)
        return jnp.einsum(
            "nkpc,nkqc->npq", left_tiles, right_tiles, preferred_element_type=jnp.float32
        )

    def in_blocks(values):
        return values.reshape((row_count // block_rows, block_rows) + values.shape[1:])

    product = lax.map(one_block, (in_blocks(amp_pos), in_blocks(int_pos), in_blocks(keep_mask)))
    return product.reshape(row_count, tile_width, tile_width)


def body(amp_tiles, int_tiles, requests, tri_amp, tri_int, tri_count):
    wanted = requests[0, 0]
    asked = lax.all_to_all(wanted, "own", split_axis=0, concat_axis=0, tiled=True)
    send_amp = select_tiles(amp_tiles, asked[:, 0])
    send_int = select_tiles(int_tiles, asked[:, 1])
    got_amp, got_int = (
        lax.all_to_all(send_amp, "own", split_axis=0, concat_axis=0, tiled=True),
        lax.all_to_all(send_int, "own", split_axis=0, concat_axis=0, tiled=True),
    )
    flat_amp = got_amp.reshape((-1,) + got_amp.shape[2:])
    flat_int = got_int.reshape((-1,) + got_int.shape[2:])
    amp_pos = tri_amp[:, 0]
    int_pos = tri_int[:, 0]
    counts = tri_count[:, 0]
    return lax.psum_scatter(
        contract_rows(flat_amp, flat_int, amp_pos, int_pos, counts),
        "red",
        scatter_dimension=0,
        tiled=True,
    )


def solution(mesh):
    placed = (
        P(("own", "red"), None, None),
        P(("own", "red"), None, None),
        P("own", "red", None, None, None),
        P("own", "red", None),
        P("own", "red", None),
        P("own", "red"),
    )
    return jax.shard_map(
        body, mesh=mesh, in_specs=placed, out_specs=P(("own", "red"), None, None), check_vma=False
    )
```

profile of v0, /device:TPU:0, one launch (start us, length us, event | category | flops | bytes accessed | tf_op | source)
XLA Modules:
  0.0 334.4 jit_solution(1003385836091410101)
XLA Ops:
  6.5 0.0 copy-start
  6.5 13.9 %all_to_all.15 = s32[8,2,8]{2,1,0:T(2,128)S(1)} all-to-all(s32[8,2,8]{2,1,0:T(2,128)} %bitcast.96), channel_id=1, replica_groups=mesh['own'=8,'red'=4] {'own'}, dimensions={0} | all-to-all | bytes 1024 | tf_op jit(solution)/shard_map/all_to_all | solution.py:52
  20.5 0.1 reshape.93
  20.6 0.0 copy-done
  20.6 2.2 gather_fusion.1
  22.8 4.2 %copy_select_fusion = bf16[8,8,128,128]{3,1,2,0:T(8,128)(2,1)} fusion(bf16[8,8,128,128]{3,2,1,0:T(8,128)(2,1)} %bitcast.89, pred[8,8]{1,0:T(8,128)(4,1)S(1)} %compare_bitcast_fusion), kind=kLoop, calls=%fused_computation.21 | loop fusion | flops 1048576 | bytes 4194368 | tf_op jit(solution)/shard_map/jit(_where)/select_n | solution.py:12
  27.0 3.6 %all-to-all-start.2 = ((bf16[8,8,128,128]{3,1,2,0:T(8,128)(2,1)}), bf16[8,8,128,128]{3,1,2,0:T(8,128)(2,1)S(1)}, u32[]{:S(2)}, u32[]{:S(2)}) async-start(bf16[8,8,128,128]{3,1,2,0:T(8,128)(2,1)} %copy_select_fusion), calls=%async_computation.2 | async-start | bytes 4194304 | tf_op jit(solution)/shard_map/all_to_all | solution.py:57
  30.6 0.1 reshape.85
  30.7 3.7 %gather_fusion = bf16[64,128,128]{2,1,0:T(8,128)(2,1)} fusion(bf16[64,128,128]{2,1,0:T(8,128)(2,1)} %param.8, s32[1024]{0:T(1024)S(1)} %pad_clamp_fusion.1), kind=kCustom, calls=%fused_computation | custom fusion | bytes 4194560 | tf_op jit(solution)/shard_map/gather | solution.py:11
  34.5 4.3 %copy_select_fusion.1 = bf16[8,8,128,128]{3,1,2,0:T(8,128)(2,1)} fusion(bf16[8,8,128,128]{3,2,1,0:T(8,128)(2,1)} %bitcast.88, pred[8,8]{1,0:T(8,128)(4,1)S(1)} %compare_bitcast_fusion.1), kind=kLoop, calls=%fused_computation.22 | loop fusion | flops 1048576 | bytes 4194368 | tf_op jit(solution)/shard_map/jit(_where)/select_n | solution.py:12
  38.7 0.0 copy-start.2
  38.7 38.9 %all-to-all-done.2 = bf16[8,8,128,128]{3,1,2,0:T(8,128)(2,1)S(1)} async-done(((bf16[8,8,128,128]{3,1,2,0:T(8,128)(2,1)}), bf16[8,8,128,128]{3,1,2,0:T(8,128)(2,1)S(1)}, u32[]{:S(2)}, u32[]{:S(2)}) %all-to-all-start.2) | async-done | bytes 2097184 | tf_op jit(solution)/shard_map/all_to_all | solution.py:57
  77.6 4.3 %all-to-all-start.1 = ((bf16[8,8,128,128]{3,1,2,0:T(8,128)(2,1)}), bf16[8,8,128,128]{3,1,2,0:T(8,128)(2,1)}, u32[]{:S(2)}, u32[]{:S(2)}) async-start(bf16[8,8,128,128]{3,1,2,0:T(8,128)(2,1)} %copy_select_fusion.1), calls=%async_computation.1 | async-start | bytes 4194304 | tf_op jit(solution)/shard_map/all_to_all | solution.py:56
  82.0 0.0 reduce-scatter.2.cloned.1.call-start
  82.0 0.6 broadcast.105
  82.6 0.0 copy-done.2
  82.6 0.7 reduce.3
  83.3 0.1 lt.34
  83.4 0.1 iota_compare_fusion.3
  83.5 46.3 %all-to-all-done.1 = bf16[8,8,128,128]{3,1,2,0:T(8,128)(2,1)} async-done(((bf16[8,8,128,128]{3,1,2,0:T(8,128)(2,1)}), bf16[8,8,128,128]{3,1,2,0:T(8,128)(2,1)}, u32[]{:S(2)}, u32[]{:S(2)}) %all-to-all-start.1) | async-done | bytes 2097184 | tf_op jit(solution)/shard_map/all_to_all | solution.py:56
  129.8 167.1 %while.12 = (s32[]{:T(128)}, f32[4,8,128,128]{3,2,1,0:T(8,128)}, s32[4,8,64]{2,1,0:T(8,128)}, pred[4,8,64]{2,1,0:T(8,128)(4,1)S(1)}, bf16[64,16384]{1,0:T(8,128)...) while((s32[]{:T(128)}, f32[4,8,128,128]{3,2,1,0:T(8,128)}, ...), condition=%wide.region_1.2_spmd.clone.clone, body=%wide.region_0.1_spmd.clone.clone.sunk | while | flops 4311842816 | bytes 138950752 | solution.py:46
  129.8 0.7 dynamic-slice_bitcast_fusion.5
  130.5 6.4 %convolution_convert_fusion.5 = bf16[8,64,16384]{2,1,0:T(8,128)(2,1)S(1)} fusion(bf16[64,16384]{1,0:T(8,128)(2,1)} %get-tuple-element.172, s32[8,64]{1,0:T(8,128)S(1)} %get-tuple-element.151, pred[8,64]{1,0:T(8,128)(4,1)S(1)} %dynamic-slice_bitcast_fusion.6), kind=kOutput, calls=%fused_computation.4.clone.1 | convolution fusion | flops 1082195968 | bytes 18876928 | tf_op jit(solution)/shard_map/while/body/eval_jaxpr/nkm,mx->nkx/dot_general | solution.py:31
  136.9 8.3 %copy.27 = bf16[64,8,128,128]{3,2,1,0:T(8,128)(2,1)} copy(bf16[64,8,128,128]{3,1,2,0:T(8,128)(2,1)S(1)} %bitcast.83) | data formatting | bytes 33554432 | tf_op jit(solution)/shard_map/while
  145.2 4.8 %convolution_convert_fusion.4 = bf16[8,64,16384]{2,1,0:T(8,128)(2,1)S(1)} fusion(bf16[64,16384]{1,0:T(8,128)(2,1)S(1)} %get-tuple-element.174, s32[8,64]{1,0:T(8,128)S(1)} %get-tuple-element.150), kind=kOutput, calls=%fused_computation.3.clone.1 | convolution fusion | flops 1082163200 | bytes 18876416 | tf_op jit(solution)/shard_map/while/body/eval_jaxpr/nkm,mx->nkx/dot_general | solution.py:34
  150.0 8.3 %copy.26 = bf16[64,8,128,128]{3,2,1,0:T(8,128)(2,1)} copy(bf16[64,8,128,128]{3,1,2,0:T(8,128)(2,1)S(1)} %bitcast.86) | data formatting | bytes 33554432 | tf_op jit(solution)/shard_map/while
  158.3 13.3 %fusion.30 = f32[4,8,128,128]{3,2,1,0:T(8,128)} fusion(f32[4,8,128,128]{3,2,1,0:T(8,128)} %get-tuple-element.161, s32[]{:T(128)} %get-tuple-element.160, bf16[8,64,128,128]{3,2,1,0:T(8,128)(2,1)} %bitcast.85, bf16[8,64,128,128]{3,2,1,0:T(8,128)(2,1)} %bitcast.84), kind=kOutput, calls=%fused_computation.11.clone.1 | convolution fusion | flops 2147483648 | bytes 34079232 | tf_op jit(solution)/shard_map/while/body/eval_jaxpr/nkpc,nkqc->npq/dot_general | solution.py:39
  171.6 0.7 dynamic-slice_bitcast_fusion.5
  172.3 6.4 %convolution_convert_fusion.5 = bf16[8,64,16384]{2,1,0:T(8,128)(2,1)S(1)} fusion(bf16[64,16384]{1,0:T(8,128)(2,1)} %get-tuple-element.172, s32[8,64]{1,0:T(8,128)S(1)} %get-tuple-element.151, pred[8,64]{1,0:T(8,128)(4,1)S(1)} %dynamic-slice_bitcast_fusion.6), kind=kOutput, calls=%fused_computation.4.clone.1 | convolution fusion | flops 1082195968 | bytes 18876928 | tf_op jit(solution)/shard_map/while/body/eval_jaxpr/nkm,mx->nkx/dot_general | solution.py:31
  178.7 8.3 %copy.27 = bf16[64,8,128,128]{3,2,1,0:T(8,128)(2,1)} copy(bf16[64,8,128,128]{3,1,2,0:T(8,128)(2,1)S(1)} %bitcast.83) | data formatting | bytes 33554432 | tf_op jit(solution)/shard_map/while
  187.0 4.8 %convolution_convert_fusion.4 = bf16[8,64,16384]{2,1,0:T(8,128)(2,1)S(1)} fusion(bf16[64,16384]{1,0:T(8,128)(2,1)S(1)} %get-tuple-element.174, s32[8,64]{1,0:T(8,128)S(1)} %get-tuple-element.150), kind=kOutput, calls=%fused_computation.3.clone.1 | convolution fusion | flops 1082163200 | bytes 18876416 | tf_op jit(solution)/shard_map/while/body/eval_jaxpr/nkm,mx->nkx/dot_general | solution.py:34
  191.7 8.3 %copy.26 = bf16[64,8,128,128]{3,2,1,0:T(8,128)(2,1)} copy(bf16[64,8,128,128]{3,1,2,0:T(8,128)(2,1)S(1)} %bitcast.86) | data formatting | bytes 33554432 | tf_op jit(solution)/shard_map/while
  200.0 13.3 %fusion.30 = f32[4,8,128,128]{3,2,1,0:T(8,128)} fusion(f32[4,8,128,128]{3,2,1,0:T(8,128)} %get-tuple-element.161, s32[]{:T(128)} %get-tuple-element.160, bf16[8,64,128,128]{3,2,1,0:T(8,128)(2,1)} %bitcast.85, bf16[8,64,128,128]{3,2,1,0:T(8,128)(2,1)} %bitcast.84), kind=kOutput, calls=%fused_computation.11.clone.1 | convolution fusion | flops 2147483648 | bytes 34079232 | tf_op jit(solution)/shard_map/while/body/eval_jaxpr/nkpc,nkqc->npq/dot_general | solution.py:39
  213.3 0.7 dynamic-slice_bitcast_fusion.5
  214.0 6.4 %convolution_convert_fusion.5 = bf16[8,64,16384]{2,1,0:T(8,128)(2,1)S(1)} fusion(bf16[64,16384]{1,0:T(8,128)(2,1)} %get-tuple-element.172, s32[8,64]{1,0:T(8,128)S(1)} %get-tuple-element.151, pred[8,64]{1,0:T(8,128)(4,1)S(1)} %dynamic-slice_bitcast_fusion.6), kind=kOutput, calls=%fused_computation.4.clone.1 | convolution fusion | flops 1082195968 | bytes 18876928 | tf_op jit(solution)/shard_map/while/body/eval_jaxpr/nkm,mx->nkx/dot_general | solution.py:31
  220.4 8.3 %copy.27 = bf16[64,8,128,128]{3,2,1,0:T(8,128)(2,1)} copy(bf16[64,8,128,128]{3,1,2,0:T(8,128)(2,1)S(1)} %bitcast.83) | data formatting | bytes 33554432 | tf_op jit(solution)/shard_map/while
  228.7 4.8 %convolution_convert_fusion.4 = bf16[8,64,16384]{2,1,0:T(8,128)(2,1)S(1)} fusion(bf16[64,16384]{1,0:T(8,128)(2,1)S(1)} %get-tuple-element.174, s32[8,64]{1,0:T(8,128)S(1)} %get-tuple-element.150), kind=kOutput, calls=%fused_computation.3.clone.1 | convolution fusion | flops 1082163200 | bytes 18876416 | tf_op jit(solution)/shard_map/while/body/eval_jaxpr/nkm,mx->nkx/dot_general | solution.py:34
  233.5 8.3 %copy.26 = bf16[64,8,128,128]{3,2,1,0:T(8,128)(2,1)} copy(bf16[64,8,128,128]{3,1,2,0:T(8,128)(2,1)S(1)} %bitcast.86) | data formatting | bytes 33554432 | tf_op jit(solution)/shard_map/while
  241.8 13.3 %fusion.30 = f32[4,8,128,128]{3,2,1,0:T(8,128)} fusion(f32[4,8,128,128]{3,2,1,0:T(8,128)} %get-tuple-element.161, s32[]{:T(128)} %get-tuple-element.160, bf16[8,64,128,128]{3,2,1,0:T(8,128)(2,1)} %bitcast.85, bf16[8,64,128,128]{3,2,1,0:T(8,128)(2,1)} %bitcast.84), kind=kOutput, calls=%fused_computation.11.clone.1 | convolution fusion | flops 2147483648 | bytes 34079232 | tf_op jit(solution)/shard_map/while/body/eval_jaxpr/nkpc,nkqc->npq/dot_general | solution.py:39
  255.1 0.7 dynamic-slice_bitcast_fusion.5
  255.8 6.4 %convolution_convert_fusion.5 = bf16[8,64,16384]{2,1,0:T(8,128)(2,1)S(1)} fusion(bf16[64,16384]{1,0:T(8,128)(2,1)} %get-tuple-element.172, s32[8,64]{1,0:T(8,128)S(1)} %get-tuple-element.151, pred[8,64]{1,0:T(8,128)(4,1)S(1)} %dynamic-slice_bitcast_fusion.6), kind=kOutput, calls=%fused_computation.4.clone.1 | convolution fusion | flops 1082195968 | bytes 18876928 | tf_op jit(solution)/shard_map/while/body/eval_jaxpr/nkm,mx->nkx/dot_general | solution.py:31
  262.2 8.3 %copy.27 = bf16[64,8,128,128]{3,2,1,0:T(8,128)(2,1)} copy(bf16[64,8,128,128]{3,1,2,0:T(8,128)(2,1)S(1)} %bitcast.83) | data formatting | bytes 33554432 | tf_op jit(solution)/shard_map/while
  270.5 4.8 %convolution_convert_fusion.4 = bf16[8,64,16384]{2,1,0:T(8,128)(2,1)S(1)} fusion(bf16[64,16384]{1,0:T(8,128)(2,1)S(1)} %get-tuple-element.174, s32[8,64]{1,0:T(8,128)S(1)} %get-tuple-element.150), kind=kOutput, calls=%fused_computation.3.clone.1 | convolution fusion | flops 1082163200 | bytes 18876416 | tf_op jit(solution)/shard_map/while/body/eval_jaxpr/nkm,mx->nkx/dot_general | solution.py:34
  275.3 8.3 %copy.26 = bf16[64,8,128,128]{3,2,1,0:T(8,128)(2,1)} copy(bf16[64,8,128,128]{3,1,2,0:T(8,128)(2,1)S(1)} %bitcast.86) | data formatting | bytes 33554432 | tf_op jit(solution)/shard_map/while
  283.6 13.3 %fusion.30 = f32[4,8,128,128]{3,2,1,0:T(8,128)} fusion(f32[4,8,128,128]{3,2,1,0:T(8,128)} %get-tuple-element.161, s32[]{:T(128)} %get-tuple-element.160, bf16[8,64,128,128]{3,2,1,0:T(8,128)(2,1)} %bitcast.85, bf16[8,64,128,128]{3,2,1,0:T(8,128)(2,1)} %bitcast.84), kind=kOutput, calls=%fused_computation.11.clone.1 | convolution fusion | flops 2147483648 | bytes 34079232 | tf_op jit(solution)/shard_map/while/body/eval_jaxpr/nkpc,nkqc->npq/dot_general | solution.py:39
  296.9 0.0 copy-start.1
  296.9 0.0 reduce-scatter.2.cloned.1.call-update
  296.9 30.6 %reduce-scatter.2.cloned.1.call-done = f32[8,128,128]{2,1,0:T(8,128)} async-done(((f32[32,128,128]{2,1,0:T(8,128)}), f32[8,128,128]{2,1,0:T(8,128)}) %reduce-scatter.2.cloned.1.call-update) | async-done | bytes 524304 | tf_op jit(solution)/shard_map/reduce_scatter | solution.py:64
  327.6 0.0 copy-done.1
  (12 shorter events, 0.1 us)
Async XLA Ops:
  6.5 14.1 %copy-start = (bf16[64,128,128]{2,1,0:T(8,128)(2,1)S(1)}, bf16[64,128,128]{2,1,0:T(8,128)(2,1)}, u32[]{:S(2)}) copy-start(bf16[64,128,128]{2,1,0:T(8,128)(2,1)} %param.9) | copy-start | bytes 6291460
  27.0 50.6 %all-to-all-start.2 = ((bf16[8,8,128,128]{3,1,2,0:T(8,128)(2,1)}), bf16[8,8,128,128]{3,1,2,0:T(8,128)(2,1)S(1)}, u32[]{:S(2)}, u32[]{:S(2)}) async-start(bf16[8,8,128,128]{3,1,2,0:T(8,128)(2,1)} %copy_select_fusion), calls=%async_computation.2 | async-start | bytes 4194304 | tf_op jit(solution)/shard_map/all_to_all | solution.py:57
  38.7 43.9 %copy-start.2 = (s32[32,1]{0,1:T(1,128)S(1)}, s32[32,1]{0,1:T(1,128)}, u32[]{:S(2)}) copy-start(s32[32,1]{0,1:T(1,128)} %param.13) | copy-start | bytes 388
  77.6 52.2 %all-to-all-start.1 = ((bf16[8,8,128,128]{3,1,2,0:T(8,128)(2,1)}), bf16[8,8,128,128]{3,1,2,0:T(8,128)(2,1)}, u32[]{:S(2)}, u32[]{:S(2)}) async-start(bf16[8,8,128,128]{3,1,2,0:T(8,128)(2,1)} %copy_select_fusion.1), calls=%async_computation.1 | async-start | bytes 4194304 | tf_op jit(solution)/shard_map/all_to_all | solution.py:56
  82.0 245.6 %reduce-scatter.2.cloned.1.call-start = ((), (), s32[]{:S(2)}) async-start(), calls=%async_computation.4 | async-start | bytes 2621440 | tf_op jit(solution)/shard_map/reduce_scatter | solution.py:64
  296.9 30.7 %copy-start.1 = (bf16[64,128,128]{2,1,0:T(8,128)(2,1)S(1)}, bf16[64,128,128]{2,1,0:T(8,128)(2,1)}, u32[]{:S(2)}) copy-start(bf16[64,128,128]{2,1,0:T(8,128)(2,1)} %param.9) | copy-start | bytes 6291460
Sparse Core Ops, SparseCore 0:
  297.1 30.4 reduce-scatter.1
where the time goes:
time: 335 us; the launch traced here: 334 us
  waiting for transfers between devices  116 us (35%)
  matrix products  97.8 us (29%)
  local copies, waits for them, and re-layouts  76 us (23%)
  blocking collectives  13.9 us (4%)
  between operations  13.5 us (4%)
  other arithmetic  9.34 us (3%)
  starting transfers between devices  7.99 us (2%)
    while x8, local copies, waits for them, and re-layouts  66.4 us
    dot_general x4, matrix products, one_block(): jnp.einsum('nkpc,nkqc->npq', left_tiles, right_tiles, preferred_element_t...  53.2 us
    all_to_all x1, waiting for transfers between devices, body(): lax.all_to_all(send_amp, 'own', split_axis=0, concat_axis=0, tiled=True)  46.3 us
    all_to_all x1, waiting for transfers between devices, body(): lax.all_to_all(send_int, 'own', split_axis=0, concat_axis=0, tiled=True)  38.9 us
    reduce_scatter x1, waiting for transfers between devices, body(): lax.psum_scatter(contract_rows(flat_amp, flat_int, amp_pos, int_pos, coun...  30.6 us
    dot_general x4, matrix products, one_block(): jnp.einsum('nkm,mx->nkx', pick_amp, flat_amp, preferred_element_type=jnp....  25.5 us
    dot_general x4, matrix products, one_block(): jnp.einsum('nkm,mx->nkx', pick_int, flat_int, preferred_element_type=jnp....  19.1 us
    all_to_all x1, blocking collectives, body(): lax.all_to_all(wanted, 'own', split_axis=0, concat_axis=0, tiled=True)  13.9 us
  transfers between devices with their start and end apart: 3, of which 3 were waited for; matrix products, arithmetic and copies ran while one was open for 3% of the time, Pallas kernels for 0%

commit v1 on v0

v1 whole, which is shorter than its diff:
```python
import functools

import jax
import jax.numpy as jnp
from jax import lax
from jax.experimental import pallas as pl
from jax.experimental.pallas import tpu as pltpu
from jax.sharding import PartitionSpec as P

MESH = pl.DeviceIdType.MESH
CORES = 2
GROUP = 16


def flip_bits(value, mask):
    bit = 1
    while bit <= mask:
        if mask & bit:
            value = value + (1 - 2 * ((value // bit) % 2)) * bit
        bit *= 2
    return value


def kernel(
    n_own, n_red, cap, rows, slots,
    req_ref, amp_hbm, int_hbm, tri_amp, tri_int,
    out_ref,
    asked_vmem, asked_smem, amp_store, int_store,
    send_amp, send_int, recv_amp, recv_int, part, sib, across,
    req_send, req_recv, local_sem, tile_send, tile_recv,
    sib_send, sib_recv, across_send, across_recv,
):
    store = amp_store.shape[0]
    received = n_own * cap
    n_x = n_red // CORES
    per_dev = rows // n_red
    me = lax.axis_index("own")
    red = lax.axis_index("red")
    my_x, my_core = red // CORES, red % CORES
    sibling = my_x * CORES + (1 - my_core)

    load_amp = pltpu.make_async_copy(amp_hbm, amp_store, local_sem.at[0])
    load_int = pltpu.make_async_copy(int_hbm, int_store, local_sem.at[1])
    load_amp.start()
    load_int.start()

    barrier = pltpu.get_barrier_semaphore()
    for step in range(1, n_own):
        pl.semaphore_signal(
            barrier, inc=1, device_id={"own": flip_bits(me, step)}, device_id_type=MESH
        )
    pl.semaphore_signal(barrier, inc=1, device_id={"red": sibling}, device_id_type=MESH)
    for step in range(1, n_x):
        peer = ((my_x + step) % n_x) * CORES + my_core
        pl.semaphore_signal(barrier, inc=1, device_id={"red": peer}, device_id_type=MESH)
    pl.semaphore_wait(barrier, n_own - 1 + 1 + n_x - 1)

    steps = sorted(range(1, n_own), reverse=True)

    asks = []
    for step in steps:
        peer = flip_bits(me, step)
        copy = pltpu.make_async_remote_copy(
            src_ref=req_ref.at[peer],
            dst_ref=asked_vmem.at[me],
            send_sem=req_send.at[step],
            recv_sem=req_recv.at[step],
            device_id={"own": peer},
            device_id_type=MESH,
        )
        copy.start()
        asks.append(copy)
    asked_vmem[me] = req_ref[me]
    for copy in asks:
        copy.wait()
    to_smem = pltpu.make_async_copy(asked_vmem, asked_smem, local_sem.at[2])
    to_smem.start()
    to_smem.wait()

    def wanted(peer, kind, slot):
        number = asked_smem[peer, 0, kind * cap + slot]
        return jnp.clip(number, 0, store - 1)

    sends = []
    recv_amp[received] = jnp.zeros_like(recv_amp[received])
    for kind in range(2):
        if kind == 0:
            load_amp.wait()
        else:
            load_int.wait()
        source = (amp_store, int_store)[kind]
        outbox = (send_amp, send_int)[kind]
        inbox = (recv_amp, recv_int)[kind]
        for step in steps + [0]:
            peer = flip_bits(me, step)
            for slot in range(cap):
                tile = source[wanted(peer, kind, slot)]
                if kind == 1:
                    tile = tile.T
                if step == 0:
                    inbox[me * cap + slot] = tile
                else:
                    outbox[step, slot] = tile
            if step == 0:
                continue
            copy = pltpu.make_async_remote_copy(
                src_ref=outbox.at[step],
                dst_ref=inbox.at[pl.ds(me * cap, cap)],
                send_sem=tile_send.at[kind, step],
                recv_sem=tile_recv.at[kind, step],
                device_id={"own": peer},
                device_id_type=MESH,
            )
            copy.start()
            sends.append(copy)
    for copy in sends:
        copy.wait()

    def contract(row):
        def some(block, total):
            first = row * slots + block * GROUP
            left = jnp.concatenate(
                [recv_amp[tri_amp[first + k]] for k in range(GROUP)], axis=1
            )
            right = jnp.concatenate(
                [recv_int[tri_int[first + k]] for k in range(GROUP)], axis=0
            )
            return total + jnp.dot(left, right, preferred_element_type=jnp.float32)

        zero = jnp.zeros(part.shape[1:], jnp.float32)
        return lax.fori_loop(0, slots // GROUP, some, zero)

    def to_sibling(x, j):
        row = (x * CORES + (1 - my_core)) * per_dev + j
        return pltpu.make_async_remote_copy(
            src_ref=part.at[row],
            dst_ref=sib.at[x, j],
            send_sem=sib_send.at[x, j],
            recv_sem=sib_recv.at[x, j],
            device_id={"red": sibling},
            device_id_type=MESH,
        )

    def to_across(step, j):
        x = (my_x + step) % n_x
        row = (x * CORES + my_core) * per_dev + j
        return pltpu.make_async_remote_copy(
            src_ref=part.at[row],
            dst_ref=across.at[step - 1, j],
            send_sem=across_send.at[step - 1, j],
            recv_sem=across_recv.at[step - 1, j],
            device_id={"red": x * CORES + my_core},
            device_id_type=MESH,
        )

    for step in list(range(1, n_x)) + [0]:
        x = (my_x + step) % n_x

        def for_sibling(j, carry):
            row = (x * CORES + (1 - my_core)) * per_dev + j
            part[row] = contract(row)
            to_sibling(x, j).start()
            return carry

        lax.fori_loop(0, per_dev, for_sibling, 0)

        def for_mine(j, carry):
            row = (x * CORES + my_core) * per_dev + j
            value = contract(row)
            to_sibling(x, j).wait_recv()
            if step == 0:
                out_ref[j] = value + sib[x, j]
            else:
                part[row] = value + sib[x, j]
                to_across(step, j).start()
            return carry

        lax.fori_loop(0, per_dev, for_mine, 0)

    for step in range(1, n_x):
        def finish(j, carry):
            to_across(step, j).wait_recv()
            out_ref[j] += across[step - 1, j]
            to_across(step, j).wait_send()
            return carry

        lax.fori_loop(0, per_dev, finish, 0)
    for x in range(n_x):
        def drain(j, carry):
            to_sibling(x, j).wait_send()
            return carry

        lax.fori_loop(0, per_dev, drain, 0)


def body(n_own, n_red, amp_tiles, int_tiles, requests, tri_amp, tri_int, tri_count):
    rows, _, slots = tri_amp.shape
    cap = requests.shape[-1]
    tile = amp_tiles.shape[1:]
    store = amp_tiles.shape[0]
    received = n_own * cap
    n_x = n_red // CORES
    per_dev = rows // n_red
    wide = 128
    asked = requests[0, 0].reshape(n_own, 1, 2 * cap)
    asked = jnp.pad(asked, ((0, 0), (0, 0), (0, wide - 2 * cap)))
    live = lax.broadcasted_iota(jnp.int32, (rows, slots), 1) < tri_count
    left_at = jnp.where(live, tri_amp[:, 0], received).reshape(rows * slots)
    right_at = tri_int[:, 0].reshape(rows * slots)
    vmem = pl.BlockSpec(memory_space=pltpu.VMEM)
    smem = pl.BlockSpec(memory_space=pltpu.SMEM)
    hbm = pl.BlockSpec(memory_space=pl.ANY)
    dma = pltpu.SemaphoreType.DMA
    kind = amp_tiles.dtype
    return pl.pallas_call(
        functools.partial(kernel, n_own, n_red, cap, rows, slots),
        out_shape=jax.ShapeDtypeStruct((per_dev,) + tile, jnp.float32),
        in_specs=[vmem, hbm, hbm, smem, smem],
        out_specs=vmem,
        scratch_shapes=[
            pltpu.VMEM((n_own, 1, wide), jnp.int32),
            pltpu.SMEM((n_own, 1, wide), jnp.int32),
            pltpu.VMEM((store,) + tile, kind),
            pltpu.VMEM((store,) + tile, kind),
            pltpu.VMEM((n_own, cap) + tile, kind),
            pltpu.VMEM((n_own, cap) + tile, kind),
            pltpu.VMEM((received + 1,) + tile, kind),
            pltpu.VMEM((received,) + tile, kind),
            pltpu.VMEM((rows,) + tile, jnp.float32),
            pltpu.VMEM((n_x, per_dev) + tile, jnp.float32),
            pltpu.VMEM((n_x - 1, per_dev) + tile, jnp.float32),
            dma((n_own,)),
            dma((n_own,)),
            dma((3,)),
            dma((2, n_own)),
            dma((2, n_own)),
            dma((n_x, per_dev)),
            dma((n_x, per_dev)),
            dma((n_x - 1, per_dev)),
            dma((n_x - 1, per_dev)),
        ],
        compiler_params=pltpu.CompilerParams(
            collective_id=0, has_side_effects=True, vmem_limit_bytes=40 * 2**20
        ),
        cost_estimate=pl.CostEstimate(
            flops=2 * rows * slots * tile[0] ** 3,
            bytes_accessed=4 * store * tile[0] * tile[1],
            transcendentals=0,
        ),
    )(asked, amp_tiles, int_tiles, left_at, right_at)


def solution(mesh):
    placed = (
        P(("own", "red"), None, None),
        P(("own", "red"), None, None),
        P("own", "red", None, None, None),
        P("own", "red", None),
        P("own", "red", None),
        P("own", "red"),
    )
    return jax.shard_map(
        functools.partial(body, mesh.shape["own"], mesh.shape["red"]),
        mesh=mesh,
        in_specs=placed,
        out_specs=P(("own", "red"), None, None),
        check_vma=False,
    )
```

time: 335 us -> 151 us (0.45)
  Pallas kernels: 0 us -> 141 us
  waiting for transfers between devices: 116 us -> 0 us
  matrix products: 97.8 us -> 0 us
  local copies, waits for them, and re-layouts: 76 us -> 5.5 us
  blocking collectives: 13.9 us -> 0 us
  between operations: 13.5 us -> 0.02 us
  starting transfers between devices: 7.99 us -> 0 us
  other arithmetic: 9.34 us -> 3.55 us
    pallas_call x0 -> x1, Pallas kernels: none -> 141 us  [body(): pl.pallas_call(functools.partial(kernel, n_own, n_red, cap, rows, slots),...]
    dot_general x12 -> x0, matrix products: 97.8 us -> none  [the longest x4 53.2 us: one_block(): jnp.einsum('nkpc,nkqc->npq', left_tiles, right_tiles, preferred_element_t...]
    all_to_all x2 -> x0, waiting for transfers between devices: 85.2 us -> none  [the longest x1 46.3 us: body(): lax.all_to_all(send_amp, 'own', split_axis=0, concat_axis=0, tiled=True)]
    while x8 -> x0, local copies, waits for them, and re-layouts: 66.4 us -> none
    reduce_scatter x1 -> x0, waiting for transfers between devices: 30.6 us -> none  [body(): lax.psum_scatter(contract_rows(flat_amp, flat_int, amp_pos, int_pos, coun...]
    all_to_all x1 -> x0, blocking collectives: 13.9 us -> none  [body(): lax.all_to_all(wanted, 'own', split_axis=0, concat_axis=0, tiled=True)]
    select_n x4 -> x1, other arithmetic: 8.54 us -> 0.01 us  [body(): left_at = jnp.where(live, tri_amp[:, 0], received).reshape(rows * slots)]
    all_to_all x2 -> x0, starting transfers between devices: 7.95 us -> none  [the longest x1 4.34 us: body(): lax.all_to_all(send_amp, 'own', split_axis=0, concat_axis=0, tiled=True)]
  transfers between devices with their start and end apart: 3 -> 0, of which waited for: 3 -> 0; matrix products, arithmetic and copies ran while one was open for 3% -> 0% of each run, Pallas kernels for 0% -> 0%
where the time goes in v1:
time: 151 us; the launch traced here: 150 us
  Pallas kernels  141 us (93%)
  local copies, waits for them, and re-layouts  5.5 us (4%)
  other arithmetic  3.55 us (2%)
    pallas_call x1, Pallas kernels, body(): pl.pallas_call(functools.partial(kernel, n_own, n_red, cap, rows, slots),...  141 us
    unnamed x6, local copies, waits for them, and re-layouts  4.49 us

profile of v1, /device:TPU:0, one launch (start us, length us, event | category | flops | bytes accessed | tf_op | source)
XLA Modules:
  0.0 150.3 jit_solution(5662384378376737946)
XLA Ops:
  0.0 0.8 reshape_squeeze.6
  0.8 0.7 iota_compare_fusion
  1.5 0.1 lt.17
  1.6 0.5 broadcast.12
  2.1 1.4 reduce.6
  3.5 0.1 squeeze.3
  3.6 1.4 reduce.7
  5.0 0.1 reshape_squeeze.7.tri_int
  5.1 0.0 copy-start
  5.1 1.6 %copy-done = bf16[64,128,128]{2,1,0:T(8,128)(2,1)S(1)} copy-done((bf16[64,128,128]{2,1,0:T(8,128)(2,1)S(1)}, bf16[64,128,128]{2,1,0:T(8,128)(2,1)}, u32[]{:S(2)}) %copy-start) | copy-done | bytes 2097176
  6.7 0.0 copy-start.1
  6.7 1.6 %copy-done.1 = bf16[64,128,128]{2,1,0:T(8,128)(2,1)S(1)} copy-done((bf16[64,128,128]{2,1,0:T(8,128)(2,1)S(1)}, bf16[64,128,128]{2,1,0:T(8,128)(2,1)}, u32[]{:S(2)}) %copy-start.1) | copy-done | bytes 2097176
  8.3 141.3 %shard_map.64 = f32[8,128,128]{2,1,0:T(8,128)S(1)} custom-call(s32[8,1,128]{2,1,0:T(1,128)S(1)} %pad.4.req_ref, bf16[64,128,128]{2,1,0:T(8,128)(2,1)S(1)} %copy-done, bf16[64,128,128]{2,1,0:T(8,128)(2,1)S(1)} %copy-done.1, s32[2048]{0:T(1024)S(1)} %broadcast_select_fusion.tri_amp, s32[2048]{0:T(1024)S(1)} %reshape_squeeze.7.tri_int), custom_call_target="tpu_custom_call" | custom-call | flops 8589934592 | bytes 4194304 | tf_op jit(solution)/shard_map/pallas_call | solution.py:215
  149.5 0.8 copy.9
  (2 shorter events, 0.0 us)
Async XLA Ops:
  5.1 1.6 %copy-start = (bf16[64,128,128]{2,1,0:T(8,128)(2,1)S(1)}, bf16[64,128,128]{2,1,0:T(8,128)(2,1)}, u32[]{:S(2)}) copy-start(bf16[64,128,128]{2,1,0:T(8,128)(2,1)} %amp_hbm.1) | copy-start | bytes 6291460
  6.7 1.6 %copy-start.1 = (bf16[64,128,128]{2,1,0:T(8,128)(2,1)S(1)}, bf16[64,128,128]{2,1,0:T(8,128)(2,1)}, u32[]{:S(2)}) copy-start(bf16[64,128,128]{2,1,0:T(8,128)(2,1)} %int_hbm.1) | copy-start | bytes 6291460

commit v2 on v1

v2 whole, which is shorter than its diff:
```python
import functools

import jax
import jax.numpy as jnp
from jax import lax
from jax.experimental import pallas as pl
from jax.experimental.pallas import tpu as pltpu
from jax.sharding import PartitionSpec as P

MESH = pl.DeviceIdType.MESH
CORES = 2
EARLY_GROUP = 32
LATE_GROUP = 8


def flip_bits(value, mask):
    bit = 1
    while bit <= mask:
        if mask & bit:
            value = value + (1 - 2 * ((value // bit) % 2)) * bit
        bit *= 2
    return value


def product(amp_list, int_list):
    left = jnp.concatenate(amp_list, axis=1)
    right = jnp.concatenate(int_list, axis=0)
    return jnp.dot(left, right, preferred_element_type=jnp.float32)


def exchange_kernel(
    n_own, cap, rows, slots,
    req_ref, amp_hbm, int_hbm, tri_amp, tri_int, counts, amp_vec, int_vec,
    recv_amp, far_int, part, late,
    near_int, asked_vmem, asked_smem, amp_store, int_store, send_amp, send_int,
    req_send, req_recv, local_sem, tile_send, tile_recv,
):
    store = amp_store.shape[0]
    received = n_own * cap
    half_own = n_own // 2
    half_slots = half_own * cap
    me = lax.axis_index("own")
    my_half = me // half_own

    load_amp = pltpu.make_async_copy(amp_hbm, amp_store, local_sem.at[0])
    load_int = pltpu.make_async_copy(int_hbm, int_store, local_sem.at[1])
    load_amp.start()
    load_int.start()

    barrier = pltpu.get_barrier_semaphore()
    for step in range(1, n_own):
        pl.semaphore_signal(
            barrier, inc=1, device_id={"own": flip_bits(me, step)}, device_id_type=MESH
        )
    pl.semaphore_wait(barrier, n_own - 1)

    asks = []
    for step in range(n_own - 1, 0, -1):
        peer = flip_bits(me, step)
        copy = pltpu.make_async_remote_copy(
            src_ref=req_ref.at[peer],
            dst_ref=asked_vmem.at[me],
            send_sem=req_send.at[step],
            recv_sem=req_recv.at[step],
            device_id={"own": peer},
            device_id_type=MESH,
        )
        copy.start()
        asks.append(copy)
    asked_vmem[me] = req_ref[me]
    for copy in asks:
        copy.wait()
    to_smem = pltpu.make_async_copy(asked_vmem, asked_smem, local_sem.at[2])
    to_smem.start()
    to_smem.wait()

    far = list(range(n_own - 1, half_own - 1, -1))
    near = list(range(half_own - 1, 0, -1))
    order = []
    for index, step in enumerate(far):
        order.append((0, step))
        if index < len(near):
            order.append((0, near[index]))
    for index, step in enumerate(far):
        if index < len(near):
            order.append((1, near[index]))
        order.append((1, step))

    def pack(kind, step, slot):
        peer = flip_bits(me, step)
        number = asked_smem[peer, kind, slot]
        source = (amp_store, int_store)[kind]
        tile = source[jnp.clip(number, 0, store - 1)]
        return tile.T if kind == 1 else tile

    my_place = (me % half_own) * cap
    recv_amp[received] = jnp.zeros_like(recv_amp[received])
    loaded = [False, False]
    copies = {}
    for kind, step in order:
        if not loaded[kind]:
            (load_amp, load_int)[kind].wait()
            loaded[kind] = True
        outbox = (send_amp, send_int)[kind]
        for slot in range(cap):
            outbox[step, slot] = pack(kind, step, slot)
        if kind == 0:
            inbox = recv_amp.at[pl.ds(me * cap, cap)]
        elif step >= half_own:
            inbox = far_int.at[pl.ds(my_place, cap)]
        else:
            inbox = near_int.at[pl.ds(my_place, cap)]
        copy = pltpu.make_async_remote_copy(
            src_ref=outbox.at[step],
            dst_ref=inbox,
            send_sem=tile_send.at[kind, step],
            recv_sem=tile_recv.at[kind, step],
            device_id={"own": flip_bits(me, step)},
            device_id_type=MESH,
        )
        copy.start()
        copies[kind, step] = copy
    for slot in range(cap):
        recv_amp[me * cap + slot] = pack(0, 0, slot)
        near_int[my_place + slot] = pack(1, 0, slot)

    wide = late.shape[-1]
    row_at = lax.broadcasted_iota(jnp.int32, (rows, slots), 0)
    slot_at = lax.broadcasted_iota(jnp.int32, (rows, slots), 1)
    live = jnp.zeros((rows, slots), jnp.int32)
    for row in range(rows):
        live = jnp.where(row_at == row, counts[row], live)
    amp_at = amp_vec[:, 0, :]
    int_at = int_vec[:, 0, :]
    is_late = (slot_at < live) & ((int_at // half_slots) != my_half)
    late_one = jnp.where(is_late, 1.0, 0.0).astype(jnp.float32)
    before = jnp.where(
        lax.broadcasted_iota(jnp.int32, (slots, slots), 0)
        < lax.broadcasted_iota(jnp.int32, (slots, slots), 1),
        1.0, 0.0,
    ).astype(jnp.float32)
    rank = jnp.dot(late_one, before, preferred_element_type=jnp.float32).astype(jnp.int32)
    rank = jnp.where(is_late, rank, wide)
    place = lax.broadcasted_iota(jnp.int32, (rows, wide), 1)
    total = jnp.sum(late_one, axis=1, keepdims=True).astype(jnp.int32)
    amp_list = jnp.where(place == slots, total, received)
    int_list = jnp.zeros((rows, wide), jnp.int32)
    int_far = int_at % half_slots
    for k in range(slots):
        here = place == rank[:, k : k + 1]
        amp_list = jnp.where(here, amp_at[:, k : k + 1], amp_list)
        int_list = jnp.where(here, int_far[:, k : k + 1], int_list)
    late[0] = amp_list
    late[1] = int_list

    for kind, step in order:
        if kind == 0 or step < half_own:
            copies[kind, step].wait_recv()

    def one_row(row, carry):
        count = counts[row]

        def some(block, total):
            amps, ints = [], []
            for k in range(EARLY_GROUP):
                slot = block * EARLY_GROUP + k
                at = tri_int[row, 0, slot]
                early = ((at // half_slots) == my_half) & (slot < count)
                amps.append(recv_amp[jnp.where(early, tri_amp[row, 0, slot], received)])
                ints.append(near_int[at % half_slots])
            return total + product(amps, ints)

        zero = jnp.zeros(part.shape[1:], jnp.float32)
        part[row] = lax.fori_loop(0, slots // EARLY_GROUP, some, zero)
        return carry

    lax.fori_loop(0, rows, one_row, 0)

    for kind, step in order:
        if kind == 1 and step >= half_own:
            copies[kind, step].wait_recv()
    for kind, step in order:
        copies[kind, step].wait_send()


def late_kernel(rows, slots, late, recv_amp, far_int, part, out):
    def one_row(row, carry):
        count = late[0, row, slots]

        def some(block, total):
            first = block * LATE_GROUP
            amps = [recv_amp[late[0, row, first + k]] for k in range(LATE_GROUP)]
            ints = [far_int[late[1, row, first + k]] for k in range(LATE_GROUP)]
            return total + product(amps, ints)

        blocks = (count + LATE_GROUP - 1) // LATE_GROUP
        out[row] = lax.fori_loop(0, blocks, some, part[row])
        return carry

    lax.fori_loop(0, rows, one_row, 0)


def scatter_kernel(
    n_red, part, out_ref, mid, sib, across, sib_send, sib_recv, across_send, across_recv
):
    n_x = n_red // CORES
    per_dev = part.shape[0] // n_red
    red = lax.axis_index("red")
    my_x, my_core = red // CORES, red % CORES
    sibling = my_x * CORES + (1 - my_core)

    barrier = pltpu.get_barrier_semaphore()
    pl.semaphore_signal(barrier, inc=1, device_id={"red": sibling}, device_id_type=MESH)
    for step in range(1, n_x):
        peer = ((my_x + step) % n_x) * CORES + my_core
        pl.semaphore_signal(barrier, inc=1, device_id={"red": peer}, device_id_type=MESH)
    pl.semaphore_wait(barrier, n_x)

    def to_sibling(step, j):
        x = (my_x + step) % n_x
        return pltpu.make_async_remote_copy(
            src_ref=part.at[(x * CORES + (1 - my_core)) * per_dev + j],
            dst_ref=sib.at[step, j],
            send_sem=sib_send.at[step, j],
            recv_sem=sib_recv.at[step, j],
            device_id={"red": sibling},
            device_id_type=MESH,
        )

    def to_across(step, j):
        x = (my_x + step) % n_x
        return pltpu.make_async_remote_copy(
            src_ref=mid.at[step - 1, j],
            dst_ref=across.at[step - 1, j],
            send_sem=across_send.at[step - 1, j],
            recv_sem=across_recv.at[step - 1, j],
            device_id={"red": x * CORES + my_core},
            device_id_type=MESH,
        )

    order = list(range(1, n_x)) + [0]
    for step in order:
        for j in range(per_dev):
            to_sibling(step, j).start()
    for step in order:
        x = (my_x + step) % n_x
        for j in range(per_dev):
            to_sibling(step, j).wait_recv()
            value = part[(x * CORES + my_core) * per_dev + j] + sib[step, j]
            if step == 0:
                out_ref[j] = value
            else:
                mid[step - 1, j] = value
                to_across(step, j).start()
    for step in range(1, n_x):
        for j in range(per_dev):
            to_across(step, j).wait_recv()
            out_ref[j] += across[step - 1, j]
    for step in order:
        for j in range(per_dev):
            to_sibling(step, j).wait_send()
            if step:
                to_across(step, j).wait_send()


def body(n_own, n_red, amp_tiles, int_tiles, requests, tri_amp, tri_int, tri_count):
    rows, _, slots = tri_amp.shape
    cap = requests.shape[-1]
    tile = amp_tiles.shape[1:]
    store = amp_tiles.shape[0]
    received = n_own * cap
    n_x = n_red // CORES
    per_dev = rows // n_red
    kind = amp_tiles.dtype
    vmem = pl.BlockSpec(memory_space=pltpu.VMEM)
    smem = pl.BlockSpec(memory_space=pltpu.SMEM)
    hbm = pl.BlockSpec(memory_space=pl.ANY)
    dma = pltpu.SemaphoreType.DMA
    shape = jax.ShapeDtypeStruct
    partial = shape((rows,) + tile, jnp.float32)
    counts = tri_count.reshape(rows)
    recv_amp, far_int, early, late = pl.pallas_call(
        functools.partial(exchange_kernel, n_own, cap, rows, slots),
        out_shape=[
            shape((received + 1,) + tile, kind),
            shape((received // 2,) + tile, kind),
            partial,
            shape((2, rows, 2 * slots), jnp.int32),
        ],
        in_specs=[vmem, hbm, hbm, smem, smem, smem, vmem, vmem],
        out_specs=[vmem] * 4,
        scratch_shapes=[
            pltpu.VMEM((received // 2,) + tile, kind),
            pltpu.VMEM((n_own, 2, cap), jnp.int32),
            pltpu.SMEM((n_own, 2, cap), jnp.int32),
            pltpu.VMEM((store,) + tile, kind),
            pltpu.VMEM((store,) + tile, kind),
            pltpu.VMEM((n_own, cap) + tile, kind),
            pltpu.VMEM((n_own, cap) + tile, kind),
            dma((n_own,)),
            dma((n_own,)),
            dma((3,)),
            dma((2, n_own)),
            dma((2, n_own)),
        ],
        compiler_params=pltpu.CompilerParams(
            collective_id=0, has_side_effects=True, vmem_limit_bytes=40 * 2**20
        ),
    )(requests[0, 0], amp_tiles, int_tiles, tri_amp, tri_int, counts, tri_amp, tri_int)
    summed = pl.pallas_call(
        functools.partial(late_kernel, rows, slots),
        out_shape=partial,
        in_specs=[smem, vmem, vmem, vmem],
        out_specs=vmem,
        compiler_params=pltpu.CompilerParams(vmem_limit_bytes=32 * 2**20),
    )(late, recv_amp, far_int, early)
    return pl.pallas_call(
        functools.partial(scatter_kernel, n_red),
        out_shape=shape((per_dev,) + tile, jnp.float32),
        in_specs=[vmem],
        out_specs=vmem,
        scratch_shapes=[
            pltpu.VMEM((n_x - 1, per_dev) + tile, jnp.float32),
            pltpu.VMEM((n_x, per_dev) + tile, jnp.float32),
            pltpu.VMEM((n_x - 1, per_dev) + tile, jnp.float32),
            dma((n_x, per_dev)),
            dma((n_x, per_dev)),
            dma((n_x - 1, per_dev)),
            dma((n_x - 1, per_dev)),
        ],
        compiler_params=pltpu.CompilerParams(
            collective_id=1, has_side_effects=True, vmem_limit_bytes=32 * 2**20
        ),
    )(summed)


def solution(mesh):
    placed = (
        P(("own", "red"), None, None),
        P(("own", "red"), None, None),
        P("own", "red", None, None, None),
        P("own", "red", None),
        P("own", "red", None),
        P("own", "red"),
    )
    return jax.shard_map(
        functools.partial(body, mesh.shape["own"], mesh.shape["red"]),
        mesh=mesh,
        in_specs=placed,
        out_specs=P(("own", "red"), None, None),
        check_vma=False,
    )
```

time: 151 us -> 145 us (0.960)
  the two profiles are of different devices: /device:TPU:0 before, /device:TPU:31 now
where the time goes in v2:
time: 145 us; the launch traced here: 144 us
  Pallas kernels  137 us (94%)
  local copies, waits for them, and re-layouts  6.76 us (5%)
    pallas_call x1, Pallas kernels, body(): pl.pallas_call(functools.partial(exchange_kernel, n_own, cap, rows, slots...  100 us
    pallas_call x1, Pallas kernels, body(): pl.pallas_call(functools.partial(scatter_kernel, n_red), out_shape=shape(...  22.9 us
    pallas_call x1, Pallas kernels, body(): pl.pallas_call(functools.partial(late_kernel, rows, slots), out_shape=par...  13.8 us
    unnamed x13, local copies, waits for them, and re-layouts  6.76 us

profile of v2, /device:TPU:31, one launch (start us, length us, event | category | flops | bytes accessed | tf_op | source)
XLA Modules:
  0.0 143.8 jit_solution(16843081625278091142)
XLA Ops:
  0.0 0.0 copy-start
  0.0 1.6 %copy-done = bf16[64,128,128]{2,1,0:T(8,128)(2,1)S(1)} copy-done((bf16[64,128,128]{2,1,0:T(8,128)(2,1)S(1)}, bf16[64,128,128]{2,1,0:T(8,128)(2,1)}, u32[]{:S(2)}) %copy-start) | copy-done | bytes 2097176
  1.6 0.0 copy-start.1
  1.6 1.6 %copy-done.1 = bf16[64,128,128]{2,1,0:T(8,128)(2,1)S(1)} copy-done((bf16[64,128,128]{2,1,0:T(8,128)(2,1)S(1)}, bf16[64,128,128]{2,1,0:T(8,128)(2,1)}, u32[]{:S(2)}) %copy-start.1) | copy-done | bytes 2097176
  3.2 0.0 copy-start.2
  3.2 0.7 copy-done.2
  3.9 0.0 copy-start.3
  3.9 0.7 copy-done.3
  4.6 0.0 copy-start.4
  4.6 0.7 copy-done.4
  5.3 0.0 copy-start.5
  5.3 0.7 copy-done.5
  6.0 100.3 %shard_map.64 = (bf16[65,128,128]{2,1,0:T(8,128)(2,1)S(1)}, bf16[32,128,128]{2,1,0:T(8,128)(2,1)S(1)}, f32[32,128,128]{2,1,0:T(8,128)S(1)}, s32[2,32,128]{2,1,0:T(8,128)S(1)}) custom-call(s32[8,2,8]{2,1,0:T(2,128)S(1)} %bitcast.2, bf16[64,128,128]{2,1,0:T(8,128)(2,1)S(1)} %copy-done, bf16[64,128,128]{2,1,0:T(8,128)(2,1)S(1)} %copy-done.1, ...), custom_call_target="tpu_custom_call" | custom-call | tf_op jit(solution)/shard_map/pallas_call | solution.py:282
  106.3 13.8 %shard_map.65.part = f32[32,128,128]{2,1,0:T(8,128)S(1)} custom-call(s32[2,32,128]{2,1,0:T(8,128)S(1)} %get-tuple-element.9.late, bf16[65,128,128]{2,1,0:T(8,128)(2,1)S(1)} %get-tuple-element.10.recv_amp, bf16[32,128,128]{2,1,0:T(8,128)(2,1)S(1)} %get-tuple-element.11.far_int, f32[32,128,128]{2,1,0:T(8,128)S(1)} %get-tuple-element.12.part), custom_call_target="tpu_custom_call" | custom-call | tf_op jit(solution)/shard_map/pallas_call | solution.py:310
  120.1 22.9 %shard_map.66 = f32[8,128,128]{2,1,0:T(8,128)S(1)} custom-call(f32[32,128,128]{2,1,0:T(8,128)S(1)} %shard_map.65.part), custom_call_target="tpu_custom_call" | custom-call | tf_op jit(solution)/shard_map/pallas_call | solution.py:317
  143.0 0.8 copy.11
Async XLA Ops:
  0.0 1.6 %copy-start = (bf16[64,128,128]{2,1,0:T(8,128)(2,1)S(1)}, bf16[64,128,128]{2,1,0:T(8,128)(2,1)}, u32[]{:S(2)}) copy-start(bf16[64,128,128]{2,1,0:T(8,128)(2,1)} %amp_hbm.1) | copy-start | bytes 6291460
  1.6 1.6 %copy-start.1 = (bf16[64,128,128]{2,1,0:T(8,128)(2,1)S(1)}, bf16[64,128,128]{2,1,0:T(8,128)(2,1)}, u32[]{:S(2)}) copy-start(bf16[64,128,128]{2,1,0:T(8,128)(2,1)} %int_hbm.1) | copy-start | bytes 6291460
  3.2 0.7 copy-start.2
  3.9 0.7 copy-start.3
  4.6 0.7 copy-start.4
  5.3 0.7 copy-start.5
